TPU v7x, 32 devices: a whole 2x2x4 slice. The times are simulated.
32 devices in a mesh: node: 8 (over y, x, core), batch: 4 (over z).
Axes of the slice: x: 2, y: 2, z: 4, core: 2. Of those that a mesh axis runs over, the one named last changes fastest.
Arguments:
- memory: bfloat16 [65536, 128], P('node'), may hold values from -5 to 5
- src_owner: int32 [16384, 1], P(('node', 'batch')), may hold values from 0 to 7; in each aligned block of 512 rows (0 to 511, 512 to 1023, ...) at most 128 rows name the same one
- src_row: int32 [16384], P(('node', 'batch')), may hold values from 0 to 8191
- fetch_owner: int32 [16384, 11, 1], P(('node', 'batch')), may hold values from 0 to 7; in each aligned block of 5632 rows (0 to 5631, 5632 to 11263, ..., all dimensions but the last counted through in order) at most 1408 rows name the same one
- fetch_row: int32 [16384, 11], P(('node', 'batch')), may hold values from 0 to 8191
- event_tick: int32 [16384], P(('node', 'batch')), may hold values from 5000 to 9999
- source_tick: int32 [16384], P(('node', 'batch')), may hold values from 0 to 4999
- neighbour_tick: int32 [16384, 10], P(('node', 'batch')), may hold values from 0 to 4999
- time_freq: float32 [128], replicated, may hold values from 0.0001 to 0.1
- time_phase: float32 [128], replicated, may hold values from -3.140625 to 3.140625
- gru_input: bfloat16 [256, 384], replicated, may hold values from -0.375 to 0.375
- gru_hidden: bfloat16 [128, 384], replicated, may hold values from -0.5 to 0.5
- gru_bias: float32 [512], replicated, may hold values from -3 to 3
- w_query: bfloat16 [128, 128], replicated, may hold values from -0.5 to 0.5
- w_kv: bfloat16 [256, 256], replicated, may hold values from -0.375 to 0.375
- w_merge: bfloat16 [256, 128], replicated, may hold values from -0.375 to 0.375
- merge_bias: float32 [128], replicated, may hold values from -3 to 3
- out_grad: float32 [16384, 128], P(('node', 'batch')), may hold values from -0.02 to 0.02
Outputs:
- embedding: float32 [16384, 128], P(('node', 'batch'))
- memory_out: bfloat16 [65536, 128], P('node')
- grad_query: float32 [128, 128], replicated
- grad_kv: float32 [256, 256], replicated
- grad_merge: float32 [256, 128], replicated
- grad_bias: float32 [128], replicated
Inputs may be any that keep to these rules, and one draw needn't show every extreme that they name: `src_owner`: among the 512 events of one device no owner is named by more than 128 of them. `fetch_owner`: among the 512 * (11) entries of one device no owner is named by more than 1408 of them.
All inputs are finite; a program needn't handle non-finite values.
Results may differ from a plain program's by a relative error of at most 0.012.
Values may be sent and summed in bfloat16 or wider, within the bound.
A program may use at most 64 MiB of HBM per device.

v0:
```python
import math
import jax
import jax.numpy as jnp
from jax import lax
from jax.sharding import PartitionSpec as P

HEADS = 2


def time_code(delta, freq, phase):
    return jnp.cos(delta[..., None] * freq + phase)


def gru_cell(message, state, gru_input, gru_hidden, gru_bias):
    width = state.shape[-1]
    from_msg = (
        jnp.dot(message, gru_input, preferred_element_type=jnp.float32) + gru_bias[: 3 * width]
    )
    from_state = jnp.dot(state, gru_hidden, preferred_element_type=jnp.float32)
    reset = jax.nn.sigmoid(from_msg[:, :width] + from_state[:, :width])
    update = jax.nn.sigmoid(from_msg[:, width : 2 * width] + from_state[:, width : 2 * width])
    candid = jnp.tanh(
        from_msg[:, 2 * width :] + reset * (from_state[:, 2 * width :] + gru_bias[3 * width :])
    )
    return ((1.0 - update) * candid + update * state.astype(jnp.float32)).astype(jnp.bfloat16)


def last_pick(owner_ids, row_ids):
    same = (owner_ids[:, None] == owner_ids[None, :]) & (row_ids[:, None] == row_ids[None, :])
    places = jnp.arange(owner_ids.shape[0], dtype=jnp.int32)
    return jnp.max(jnp.where(same, places[None, :], jnp.int32(-1)), axis=1)


def place(owner_ids, owner_count, capacity):
    onehot = (owner_ids[:, None] == jnp.arange(owner_count, dtype=jnp.int32)[None, :]).astype(
        jnp.int32
    )
    before = jnp.cumsum(onehot, axis=0) - onehot
    return owner_ids * capacity + jnp.sum(before * onehot, axis=1)


def embed(query_w, pair_w, merge_w, bias_term, new_src, kv_in):
    att_width = query_w.shape[1]
    head_width = att_width // HEADS
    row_count = new_src.shape[0]
    nb_count = kv_in.shape[1]
    query_rows = jnp.dot(new_src, query_w.astype(jnp.bfloat16), preferred_element_type=jnp.float32)
    pairs = jnp.dot(kv_in, pair_w.astype(jnp.bfloat16), preferred_element_type=jnp.float32)
    key_rows = pairs[..., :att_width].reshape(row_count, nb_count, HEADS, head_width)
    value_rows = pairs[..., att_width:].reshape(row_count, nb_count, HEADS, head_width)
    scores = jnp.einsum(
        "ehd,enhd->ehn", query_rows.reshape(row_count, HEADS, head_width), key_rows
    ) / math.sqrt(head_width)
    scores = scores - jnp.max(scores, axis=-1, keepdims=True)
    shares = jnp.exp(scores)
    shares = shares / jnp.sum(shares, axis=-1, keepdims=True)
    mixed = (
        jnp.einsum("ehn,enhd->ehd", shares, value_rows)
        .reshape(row_count, att_width)
        .astype(jnp.bfloat16)
    )
    joined = jnp.concatenate([mixed, new_src], axis=-1)
    return jax.nn.silu(
        jnp.dot(joined, merge_w.astype(jnp.bfloat16), preferred_element_type=jnp.float32)
        + bias_term
    )


def on_device(
    memory,
    src_owner,
    src_row,
    fetch_owner,
    fetch_row,
    event_tick,
    source_tick,
    neighbour_tick,
    time_freq,
    time_phase,
    gru_input,
    gru_hidden,
    gru_bias,
    w_query,
    w_kv,
    w_merge,
    merge_bias,
    out_grad,
):
    owner_count = lax.axis_size("node")
    batch_count = lax.axis_size("batch")
    batch_place = lax.axis_index("batch")
    event_count = src_row.shape[0]
    per_event = fetch_row.shape[1]
    mem_width = memory.shape[1]
    node_local = memory.shape[0]
    far_cap = event_count * per_event * 2 // owner_count
    near_cap = event_count * 2 // owner_count
    near_owner = src_owner[:, 0]
    far_slot = place(fetch_owner.reshape(-1), owner_count, far_cap)
    near_slot = place(near_owner, owner_count, near_cap)
    far_ask = (
        jnp.zeros((owner_count * far_cap,), jnp.int32)
        .at[far_slot]
        .set(fetch_row.reshape(-1))
        .reshape(owner_count, far_cap)
    )
    near_ask = (
        jnp.zeros((owner_count * near_cap,), jnp.int32)
        .at[near_slot]
        .set(src_row + 1)
        .reshape(owner_count, near_cap)
    )
    far_got, near_got = (
        lax.all_to_all(far_ask, "node", split_axis=0, concat_axis=0, tiled=True),
        lax.all_to_all(near_ask, "node", split_axis=0, concat_axis=0, tiled=True),
    )
    near_flat = near_got.reshape(-1)
    near_live = near_flat > 0
    near_index = jnp.maximum(near_flat - 1, 0)
    far_rows = memory[far_got]
    near_rows = memory[near_index].reshape(owner_count, near_cap, mem_width)
    source_code = time_code(
        (event_tick - source_tick).astype(jnp.float32), time_freq, time_phase
    ).astype(jnp.bfloat16)
    far_back = lax.all_to_all(far_rows, "node", split_axis=0, concat_axis=0, tiled=True)
    fetched = far_back.reshape(owner_count * far_cap, mem_width)[far_slot].reshape(
        event_count, per_event, mem_width
    )
    message = jnp.concatenate([fetched[:, 0], source_code], axis=-1)
    msg_width = message.shape[1]
    outgoing = (
        jnp.zeros((owner_count * near_cap, msg_width), jnp.bfloat16)
        .at[near_slot]
        .set(message)
        .reshape(owner_count, near_cap, msg_width)
    )
    arrived = lax.all_to_all(outgoing, "node", split_axis=0, concat_axis=0, tiled=True)
    fresh = gru_cell(
        arrived.reshape(-1, msg_width),
        near_rows.reshape(-1, mem_width),
        gru_input,
        gru_hidden,
        gru_bias,
    )
    returned = lax.all_to_all(
        fresh.reshape(owner_count, near_cap, mem_width),
        "node",
        split_axis=0,
        concat_axis=0,
        tiled=True,
    )
    updated = returned.reshape(owner_count * near_cap, mem_width)[near_slot]
    sender_ids = jnp.repeat(jnp.arange(owner_count, dtype=jnp.int32), near_cap)
    slot_ids = jnp.tile(jnp.arange(near_cap, dtype=jnp.int32), owner_count)
    priority = (sender_ids * batch_count + batch_place) * near_cap + slot_ids
    packed = jnp.where(near_live, priority * node_local + near_index, jnp.int32(-1))
    all_fresh, all_keys = (
        lax.all_gather(fresh, "batch", axis=0, tiled=True),
        lax.all_gather(packed, "batch", axis=0, tiled=True),
    )
    key_live = all_keys >= 0
    key_rows = jnp.where(key_live, all_keys % node_local, node_local).astype(jnp.int32)
    best = jnp.full((node_local + 1,), -1, jnp.int32).at[key_rows].max(all_keys)
    winner = key_live & (all_keys == best[key_rows])
    target = jnp.where(winner, key_rows, node_local)
    memory_out = memory.at[target].set(all_fresh, mode="drop")
    new_src = updated[last_pick(near_owner, src_row)]
    nb_code = time_code(
        (event_tick[:, None] - neighbour_tick).astype(jnp.float32), time_freq, time_phase
    ).astype(jnp.bfloat16)
    kv_in = jnp.concatenate([fetched[:, 1:], nb_code], axis=-1)

    def forward(query_w, pair_w, merge_w, bias_term):
        return embed(query_w, pair_w, merge_w, bias_term, new_src, kv_in)

    result, pull = jax.vjp(
        forward,
        w_query.astype(jnp.float32),
        w_kv.astype(jnp.float32),
        w_merge.astype(jnp.float32),
        merge_bias,
    )
    grads = pull(out_grad)
    summed = lax.psum((grads[0], grads[1], grads[2], grads[3]), ("node", "batch"))
    return (result, memory_out, summed[0], summed[1], summed[2], summed[3])


def solution(mesh):
    return jax.shard_map(
        on_device,
        mesh=mesh,
        in_specs=(
            P("node", None),
            P(("node", "batch"), None),
            P(("node", "batch")),
            P(("node", "batch"), None, None),
            P(("node", "batch"), None),
            P(("node", "batch")),
            P(("node", "batch")),
            P(("node", "batch"), None),
            P(),
            P(),
            P(),
            P(),
            P(),
            P(),
            P(),
            P(),
            P(),
            P(("node", "batch"), None),
        ),
        out_specs=(P(("node", "batch"), None), P("node", None), P(), P(), P(), P()),
        check_vma=False,
    )
```

profile of v0, /device:TPU:1, one launch (start us, length us, event | category | flops | bytes accessed | tf_op | source)
XLA Modules:
  0.0 348.3 jit_solution(14605585450725997113)
XLA Ops:
  8.0 1.6 copy.109
  9.7 0.1 copy.58
  9.8 0.2 eq.99
  10.1 0.2 eq.95
  10.3 0.1 copy.57
  10.4 0.2 mul.131
  10.7 2.4 reduce-window.16
  13.1 0.3 slice_reduce_fusion
  13.4 0.2 reduce-window.19
  13.7 0.1 copy.60
  13.9 0.2 reshape.304
  14.3 21.1 %scatter_custom_fusion = s32[11264]{0:T(1024)S(1)} fusion(s32[5632]{0:T(1024)S(1)} %fusion.43, s32[5632]{0:T(1024)S(1)} %reshape.304, s32[]{:T(128)} %constant.24.clone.1), kind=kCustom, calls=%fused_computation.91 | custom fusion | bytes 45060 | tf_op jit(solution)/shard_map/scatter | solution.py:104
  35.4 9.1 %all_to_all.36 = s32[8,1,1408]{2,1,0:T(1,128)S(1)} all-to-all(s32[8,1,1408]{2,1,0:T(1,128)S(1)} %bitcast.125), channel_id=1, replica_groups=mesh['node'=8,'batch'=4] {'node'}, dimensions={0} | all-to-all | bytes 90112 | tf_op jit(solution)/shard_map/all_to_all | solution.py:114
  44.6 39.8 %gather_fusion = bf16[11264,128]{1,0:T(8,128)(2,1)} fusion(bf16[8192,128]{1,0:T(8,128)(2,1)S(1)} %copy.109, s32[11264]{0:T(1024)S(1)} %broadcast_clamp_fusion), kind=kCustom, calls=%fused_computation | custom fusion | bytes 5812224 | tf_op jit(solution)/shard_map/gather | solution.py:120
  84.5 5.3 %all-to-all-start.1 = ((bf16[8,1408,128]{2,1,0:T(8,128)(2,1)}), bf16[8,1408,128]{2,1,0:T(8,128)(2,1)}, u32[]{:S(2)}, u32[]{:S(2)}) async-start(bf16[8,1408,128]{2,1,0:T(8,128)(2,1)} %bitcast.114), calls=%async_computation.1 | async-start | bytes 5767168 | tf_op jit(solution)/shard_map/all_to_all | solution.py:125
  89.8 1.1 reduce-window.14
  90.9 0.2 slice_reduce_fusion.1
  91.3 3.0 scatter_custom_fusion.2
  94.3 0.4 select_reduce_fusion
  94.8 0.9 cosine_convert_fusion.1
  95.7 10.1 %cosine_convert_fusion = bf16[512,10,128]{2,0,1:T(8,128)(2,1)} fusion(f32[128]{0:T(128)S(1)} %copy-done.17, f32[128]{0:T(128)S(1)} %copy-done.18, f32[512,10]{0,1:T(8,128)S(1)} %subtract_convert_fusion), kind=kLoop, calls=%fused_computation.20 | loop fusion | flops 1966080 | bytes 1332224 | tf_op jit(solution)/shard_map/convert_element_type | solution.py:170
  105.8 15.5 %all-to-all-done.1 = bf16[8,1408,128]{2,1,0:T(8,128)(2,1)} async-done(((bf16[8,1408,128]{2,1,0:T(8,128)(2,1)}), bf16[8,1408,128]{2,1,0:T(8,128)(2,1)}, u32[]{:S(2)}, u32[]{:S(2)}) %all-to-all-start.1) | async-done | bytes 2883616 | tf_op jit(solution)/shard_map/all_to_all | solution.py:125
  121.3 6.9 %all-to-all-start.3 = ((s32[8,1,128]{2,1,0:T(1,128)}), s32[8,1,128]{2,1,0:T(1,128)S(1)}, u32[]{:S(2)}, u32[]{:S(2)}) async-start(s32[8,1,128]{2,1,0:T(1,128)} %bitcast.18), calls=%async_computation.3 | async-start | bytes 8192 | tf_op jit(solution)/shard_map/all_to_all | solution.py:115
  128.2 13.4 %gather_fusion.1 = bf16[5632,128]{1,0:T(8,128)(2,1)} fusion(bf16[11264,128]{1,0:T(8,128)(2,1)} %bitcast.15, s32[6144]{0:T(1024)S(1)} %pad_clamp_fusion), kind=kCustom, calls=%fused_computation.1 | custom fusion | bytes 2906112 | tf_op jit(solution)/shard_map/gather | solution.py:126
  141.6 3.7 %reshape.238 = bf16[512,11,128]{2,1,0:T(8,128)(2,1)} reshape(bf16[5632,128]{1,0:T(8,128)(2,1)} %gather_fusion.1) | data formatting | bytes 2883584 | tf_op jit(solution)/shard_map/reshape | solution.py:126
  145.3 1.4 slice.78
  146.7 3.2 scatter_custom_fusion.1
  149.9 4.2 %all-to-all-start.2 = ((bf16[8,128,256]{2,1,0:T(8,128)(2,1)}), bf16[8,128,256]{2,1,0:T(8,128)(2,1)S(1)}, u32[]{:S(2)}, u32[]{:S(2)}) async-start(bf16[8,128,256]{2,1,0:T(8,128)(2,1)} %bitcast.16), calls=%async_computation.2 | async-start | bytes 1048576 | tf_op jit(solution)/shard_map/all_to_all | solution.py:137
  154.1 3.2 gather_fusion.2
  157.3 10.6 %all_gather.6 = s32[4096]{0:T(1024)S(1)} all-gather(s32[1024]{0:T(1024)S(1)} %get-tuple-element.24), channel_id=1, replica_groups=mesh['node'=8,'batch'=4] {'batch'}, dimensions={0}, use_global_device_ids=true | all-gather | bytes 20480 | tf_op jit(solution)/shard_map/all_gather | solution.py:159
  168.0 1.5 fusion.65
  169.5 2.6 slice.85
  172.0 1.4 copy.95
  173.4 0.4 convolution_add_fusion
  173.9 1.0 copy-done.4
  174.8 1.1 fusion.21
  175.9 7.1 %all-to-all-start.4 = ((bf16[8,128,128]{2,1,0:T(8,128)(2,1)}), bf16[8,128,128]{2,1,0:T(8,128)(2,1)S(1)}, u32[]{:S(2)}, u32[]{:S(2)}) async-start(bf16[8,128,128]{2,1,0:T(8,128)(2,1)} %bitcast.21), calls=%async_computation.4 | async-start | bytes 524288 | tf_op jit(solution)/shard_map/all_to_all | solution.py:145
  183.0 2.6 fusion.4
  185.6 2.3 copy-done.2
  188.0 0.6 all-to-all-done.4
  188.6 1.3 gather_fusion.3
  189.9 1.3 gather_fusion.4
  191.3 0.2 fusion.66
  191.5 4.0 %multiply_reduce_fusion.3 = (f32[512,2,10]{0,1,2:T(2,128)S(1)}, f32[512,10,128]{0,2,1:T(8,128)}) fusion(f32[512,2,64]{0,2,1:T(8,128)S(1)} %bitcast.119, f32[512,10,256]{0,2,1:T(8,128)} %copy-done.2), kind=kLoop, calls=%fused_computation.19 | loop fusion | flops 1300480 | bytes 5545984 | tf_op jit(solution)/shard_map/jvp(ehd,enhd->ehn)/dot_general | solution.py:51
  195.8 0.3 multiply_reduce_fusion.2
  196.1 0.1 copy.64
  196.2 0.2 copy-done.10
  196.4 0.2 copy-done.21
  196.6 1.0 fusion.62
  197.6 0.2 fusion.67
  197.8 2.6 broadcast_multiply_fusion.1
  200.6 0.9 fusion.14
  201.6 0.4 broadcast_multiply_fusion
  202.0 0.9 fusion.15
  202.9 0.4 copy-done.6
  203.3 1.6 fusion.11
  204.9 24.3 %scatter_custom_fusion.3 = s32[8193]{0:T(1024)S(1)} fusion(s32[4096]{0:T(1024)S(1)} %get-tuple-element.23, s32[4096]{0:T(1024)S(1)} %all_gather.6, s32[]{:T(128)} %constant.30.clone.1), kind=kCustom, calls=%fused_computation.96 | custom fusion | flops 4096 | bytes 32776 | tf_op jit(solution)/shard_map/scatter-max | solution.py:163
  229.2 23.0 %gather_fusion.5 = s32[4096]{0:T(1024)S(1)} fusion(s32[8193]{0:T(1024)S(1)} %scatter_custom_fusion.3, s32[4096]{0:T(1024)S(1)} %get-tuple-element.22), kind=kCustom, calls=%fused_computation.5 | custom fusion | bytes 49152 | tf_op jit(solution)/shard_map/gather | solution.py:164
  252.3 41.2 %psum.31 = f32[128]{0:T(128)} all-reduce(f32[128]{0:T(128)S(1)} %get-tuple-element.11), channel_id=1, replica_groups=mesh['node'=8,'batch'=4] {'node','batch'}, use_global_device_ids=true, to_apply=%region_21.22 | all-reduce | flops 128 | bytes 1024 | tf_op jit(solution)/shard_map/psum | solution.py:184
  293.5 12.5 %scatter_fusion = bf16[8192,128]{1,0:T(8,128)(2,1)S(1)} fusion(bf16[8192,128]{1,0:T(8,128)(2,1)S(1)} %copy.109, s32[4096]{0:T(1024)S(1)} %compare_select_fusion.2, bf16[4096,128]{1,0:T(8,128)(2,1)} %all-gather.2.cloned.1.call-done), kind=kCustom, calls=%fused_computation.10 | custom fusion | bytes 3162112 | tf_op jit(solution)/shard_map/scatter | solution.py:166
  306.0 30.2 %all-reduce.5.cloned.1.call-done = (f32[128,128]{1,0:T(8,128)}, f32[256,256]{1,0:T(8,128)}, f32[256,128]{1,0:T(8,128)}) async-done(((f32[128,128]{1,0:T(8,128)}, f32[256,256]{1,0:T(8,128)}, f32[256,128]{1,0:T(8,128)}), (f32[128,128]{1,0:T(8,128)}, f32[256,256]{1,0:T(8,128)}, f32[256,128]{1,0:T(8,128)})) %all-reduce.5.cloned.1.call-update) | async-done | bytes 458768 | tf_op jit(solution)/shard_map/psum | solution.py:184
  336.2 1.5 copy.110
  337.6 1.7 copy.111
  339.3 1.6 copy.112
  (84 shorter events, 1.2 us)
Async XLA Ops:
  8.0 165.4 %copy-start = (bf16[256,384]{1,0:T(8,128)(2,1)S(1)}, bf16[256,384]{1,0:T(8,128)(2,1)}, u32[]{:S(2)}) copy-start(bf16[256,384]{1,0:T(8,128)(2,1)} %param.28) | copy-start | bytes 589828
  8.0 1.7 copy-start.9
  8.0 5.7 %copy-start.12 = (s32[512,11]{0,1:T(8,128)S(1)}, s32[512,11]{0,1:T(8,128)}, u32[]{:S(2)}) copy-start(s32[512,11]{0,1:T(8,128)} %param.22) | copy-start | bytes 67588
  84.4 5.3 %copy-start.11 = (s32[512,1]{0,1:T(1,128)S(1)}, s32[512,1]{0,1:T(1,128)}, u32[]{:S(2)}) copy-start(s32[512,1]{0,1:T(1,128)} %param.19) | copy-start | bytes 6148
  84.4 6.8 %copy-start.15 = (s32[512]{0:T(512)S(1)}, s32[512]{0:T(512)}, u32[]{:S(2)}) copy-start(s32[512]{0:T(512)} %param.20) | copy-start | bytes 6148
  84.4 10.3 %copy-start.16 = (s32[512]{0:T(512)S(1)}, s32[512]{0:T(512)}, u32[]{:S(2)}) copy-start(s32[512]{0:T(512)} %param.23) | copy-start | bytes 6148
  84.4 10.3 %copy-start.19 = (s32[512]{0:T(512)S(1)}, s32[512]{0:T(512)}, u32[]{:S(2)}) copy-start(s32[512]{0:T(512)} %param.24) | copy-start | bytes 6148
  84.4 10.3 %copy-start.13 = (s32[512,10]{0,1:T(8,128)S(1)}, s32[512,10]{0,1:T(8,128)}, u32[]{:S(2)}) copy-start(s32[512,10]{0,1:T(8,128)} %param.25) | copy-start | bytes 61444
  84.5 10.3 %copy-start.17 = (f32[128]{0:T(128)S(1)}, f32[128]{0:T(128)}, u32[]{:S(2)}) copy-start(f32[128]{0:T(128)} %param.27) | copy-start | bytes 1540
  84.5 10.3 %copy-start.18 = (f32[128]{0:T(128)S(1)}, f32[128]{0:T(128)}, u32[]{:S(2)}) copy-start(f32[128]{0:T(128)} %param.26) | copy-start | bytes 1540
  84.5 43.7 %copy-start.20 = (f32[512]{0:T(512)S(1)}, f32[512]{0:T(512)}, u32[]{:S(2)}) copy-start(f32[512]{0:T(512)} %param.30) | copy-start | bytes 6148
  84.5 36.8 %all-to-all-start.1 = ((bf16[8,1408,128]{2,1,0:T(8,128)(2,1)}), bf16[8,1408,128]{2,1,0:T(8,128)(2,1)}, u32[]{:S(2)}, u32[]{:S(2)}) async-start(bf16[8,1408,128]{2,1,0:T(8,128)(2,1)} %bitcast.114), calls=%async_computation.1 | async-start | bytes 5767168 | tf_op jit(solution)/shard_map/all_to_all | solution.py:125
  121.3 28.5 %all-to-all-start.3 = ((s32[8,1,128]{2,1,0:T(1,128)}), s32[8,1,128]{2,1,0:T(1,128)S(1)}, u32[]{:S(2)}, u32[]{:S(2)}) async-start(s32[8,1,128]{2,1,0:T(1,128)} %bitcast.18), calls=%async_computation.3 | async-start | bytes 8192 | tf_op jit(solution)/shard_map/all_to_all | solution.py:115
  145.3 22.7 %copy-start.8 = (bf16[128,384]{1,0:T(8,128)(2,1)S(1)}, bf16[128,384]{1,0:T(8,128)(2,1)}, u32[]{:S(2)}) copy-start(bf16[128,384]{1,0:T(8,128)(2,1)} %param.29) | copy-start | bytes 294916
  149.9 23.6 %all-to-all-start.2 = ((bf16[8,128,256]{2,1,0:T(8,128)(2,1)}), bf16[8,128,256]{2,1,0:T(8,128)(2,1)S(1)}, u32[]{:S(2)}, u32[]{:S(2)}) async-start(bf16[8,128,256]{2,1,0:T(8,128)(2,1)} %bitcast.16), calls=%async_computation.2 | async-start | bytes 1048576 | tf_op jit(solution)/shard_map/all_to_all | solution.py:137
  173.4 1.4 copy-start.4
  174.8 8.2 %copy-start.7 = (bf16[256,256]{1,0:T(8,128)(2,1)S(1)}, bf16[256,256]{1,0:T(8,128)(2,1)}, u32[]{:S(2)}) copy-start(bf16[256,256]{1,0:T(8,128)(2,1)} %param.32) | copy-start | bytes 393220
  175.9 12.7 %all-to-all-start.4 = ((bf16[8,128,128]{2,1,0:T(8,128)(2,1)}), bf16[8,128,128]{2,1,0:T(8,128)(2,1)S(1)}, u32[]{:S(2)}, u32[]{:S(2)}) async-start(bf16[8,128,128]{2,1,0:T(8,128)(2,1)} %bitcast.21), calls=%async_computation.4 | async-start | bytes 524288 | tf_op jit(solution)/shard_map/all_to_all | solution.py:145
  183.0 110.5 %all-gather.2.cloned.1.call-start = ((), (), s32[]{:S(2)}) async-start(), calls=%async_computation.5 | async-start | bytes 1310720 | tf_op jit(solution)/shard_map/all_gather | solution.py:158
  185.6 2.3 copy-start.2
  187.9 3.4 copy-start.14
  187.9 148.2 %all-reduce.5.cloned.1.call-start = ((), (), s32[]{:S(2)}) async-start(), calls=%async_computation.6 | async-start | bytes 917504 | tf_op jit(solution)/shard_map/psum | solution.py:184
  191.5 4.2 %slice-start = ((f32[512,10,256]{0,2,1:T(8,128)}), f32[512,10,128]{0,2,1:T(8,128)S(1)}, s32[]{:S(2)}) async-start(f32[512,10,256]{0,2,1:T(8,128)} %copy-done.2), calls=%async_computation.7 | async-start | bytes 5242880 | tf_op jit(solution)/shard_map/jvp()/slice | solution.py:50
  195.6 0.8 copy-start.10
  195.6 1.0 copy-start.21
  195.6 1.0 copy-start.22
  197.8 3.7 %copy-start.3 = (f32[512,10,128]{0,2,1:T(8,128)S(1)}, f32[512,10,128]{0,2,1:T(8,128)}, u32[]{:S(2)}) copy-start(f32[512,10,128]{0,2,1:T(8,128)} %get-tuple-element.16) | copy-start | bytes 7864324
  201.6 1.3 copy-start.5
  201.6 1.7 copy-start.6
  306.0 34.9 %copy-start.1 = (bf16[8192,128]{1,0:T(8,128)(2,1)}, bf16[8192,128]{1,0:T(8,128)(2,1)S(1)}, u32[]{:S(2)}) copy-start(bf16[8192,128]{1,0:T(8,128)(2,1)S(1)} %scatter_fusion) | copy-start | bytes 6291460
Sparse Core Ops, SparseCore 0:
  188.1 28.9 all-gather.1
Sparse Core Ops, SparseCore 1:
  205.0 131.1 all-reduce.4
where the time goes:
time: 349 us; the launch traced here: 348 us
  local copies, waits for them, and re-layouts  140 us (40%)
  blocking collectives  60.9 us (17%)
  other arithmetic  51.9 us (15%)
  waiting for transfers between devices  46.4 us (13%)
  starting transfers between devices  23.5 us (7%)
  between operations  16 us (5%)
  matrix products  9.36 us (3%)
    psum x1, blocking collectives, on_device(): lax.psum((grads[0], grads[1], grads[2], grads[3]), ('node', 'batch'))  41.2 us
    gather x1, local copies, waits for them, and re-layouts, on_device(): far_rows = memory[far_got]  39.8 us
    psum x1, waiting for transfers between devices, on_device(): lax.psum((grads[0], grads[1], grads[2], grads[3]), ('node', 'batch'))  30.2 us
    another operation x1, other arithmetic, on_device(): best = jnp.full((node_local + 1,), -1, jnp.int32).at[key_rows].max(all_keys)  24.3 us
    gather x1, local copies, waits for them, and re-layouts, on_device(): winner = key_live & (all_keys == best[key_rows])  23 us
    scatter x1, local copies, waits for them, and re-layouts, on_device(): far_ask = jnp.zeros((owner_count * far_cap,), jnp.int32).at[far_slot].set...  21.1 us
    all_to_all x1, waiting for transfers between devices, on_device(): lax.all_to_all(far_rows, 'node', split_axis=0, concat_axis=0, tiled=True)  15.5 us
    gather x1, local copies, waits for them, and re-layouts, on_device(): far_back.reshape(owner_count * far_cap, mem_width)[far_slot]  13.4 us
  transfers between devices with their start and end apart: 6, of which 3 were waited for; matrix products, arithmetic and copies ran while one was open for 36% of the time, Pallas kernels for 0%

commit v1 on v0

--- a/solution.py
+++ b/solution.py
@@ -181,7 +181,7 @@
         merge_bias,
     )
     grads = pull(out_grad)
-    summed = lax.psum((grads[0], grads[1], grads[2], grads[3]), ("node", "batch"))
+    summed = lax.psum(lax.psum((grads[0], grads[1], grads[2], grads[3]), "batch"), "node")
     return (result, memory_out, summed[0], summed[1], summed[2], summed[3])
 
 

time: 349 us -> 330 us (0.946)
  blocking collectives: 60.9 us -> 45.3 us
    psum x1 -> x2, blocking collectives: 41.2 us -> 25.6 us  [the longest x1 17.4 us: on_device(): lax.psum(lax.psum((grads[0], grads[1], grads[2], grads[3]), 'batch'), 'no...]
    psum x1 -> x2, waiting for transfers between devices: 30.2 us -> 29.1 us  [the longest x1 26.3 us: on_device(): lax.psum((grads[0], grads[1], grads[2], grads[3]), 'batch')]
  transfers between devices with their start and end apart: 6 -> 7, of which waited for: 3 -> 4; matrix products, arithmetic and copies ran while one was open for 36% -> 33% of each run, Pallas kernels for 0% -> 0%
where the time goes in v1:
time: 330 us; the launch traced here: 328 us
  local copies, waits for them, and re-layouts  140 us (42%)
  other arithmetic  51.9 us (16%)
  waiting for transfers between devices  46.1 us (14%)
  blocking collectives  45.3 us (14%)
  starting transfers between devices  20.8 us (6%)
  between operations  14.3 us (4%)
  matrix products  9.36 us (3%)
    gather x1, local copies, waits for them, and re-layouts, on_device(): far_rows = memory[far_got]  39.8 us
    psum x1, waiting for transfers between devices, on_device(): lax.psum((grads[0], grads[1], grads[2], grads[3]), 'batch')  26.3 us
    another operation x1, other arithmetic, on_device(): best = jnp.full((node_local + 1,), -1, jnp.int32).at[key_rows].max(all_keys)  24.3 us
    gather x1, local copies, waits for them, and re-layouts, on_device(): winner = key_live & (all_keys == best[key_rows])  23 us
    scatter x1, local copies, waits for them, and re-layouts, on_device(): far_ask = jnp.zeros((owner_count * far_cap,), jnp.int32).at[far_slot].set...  21.1 us
    psum x1, blocking collectives, on_device(): lax.psum(lax.psum((grads[0], grads[1], grads[2], grads[3]), 'batch'), 'no...  17.4 us
    all_to_all x1, waiting for transfers between devices, on_device(): lax.all_to_all(far_rows, 'node', split_axis=0, concat_axis=0, tiled=True)  15.5 us
    gather x1, local copies, waits for them, and re-layouts, on_device(): far_back.reshape(owner_count * far_cap, mem_width)[far_slot]  13.4 us
  transfers between devices with their start and end apart: 7, of which 4 were waited for; matrix products, arithmetic and copies ran while one was open for 33% of the time, Pallas kernels for 0%

profile of v1, /device:TPU:1, one launch (start us, length us, event | category | flops | bytes accessed | tf_op | source)
XLA Modules:
  0.0 328.0 jit_solution(12235207125847414358)
XLA Ops:
  7.2 1.6 copy.112
  8.9 0.1 copy.58
  9.0 0.2 eq.99
  9.2 0.2 eq.95
  9.6 0.2 mul.131
  9.9 2.4 reduce-window.16
  12.2 0.3 slice_reduce_fusion
  12.5 0.2 reduce-window.19
  13.0 0.2 reshape.304
  13.4 21.1 %scatter_custom_fusion = s32[11264]{0:T(1024)S(1)} fusion(s32[5632]{0:T(1024)S(1)} %fusion.43, s32[5632]{0:T(1024)S(1)} %reshape.304, s32[]{:T(128)} %constant.24.clone.1), kind=kCustom, calls=%fused_computation.91 | custom fusion | bytes 45060 | tf_op jit(solution)/shard_map/scatter | solution.py:104
  34.6 9.1 %all_to_all.36 = s32[8,1,1408]{2,1,0:T(1,128)S(1)} all-to-all(s32[8,1,1408]{2,1,0:T(1,128)S(1)} %bitcast.125), channel_id=1, replica_groups=mesh['node'=8,'batch'=4] {'node'}, dimensions={0} | all-to-all | bytes 90112 | tf_op jit(solution)/shard_map/all_to_all | solution.py:114
  43.8 39.8 %gather_fusion = bf16[11264,128]{1,0:T(8,128)(2,1)} fusion(bf16[8192,128]{1,0:T(8,128)(2,1)S(1)} %copy.112, s32[11264]{0:T(1024)S(1)} %broadcast_clamp_fusion), kind=kCustom, calls=%fused_computation | custom fusion | bytes 5812224 | tf_op jit(solution)/shard_map/gather | solution.py:120
  83.7 5.3 %all-to-all-start.1 = ((bf16[8,1408,128]{2,1,0:T(8,128)(2,1)}), bf16[8,1408,128]{2,1,0:T(8,128)(2,1)}, u32[]{:S(2)}, u32[]{:S(2)}) async-start(bf16[8,1408,128]{2,1,0:T(8,128)(2,1)} %bitcast.114), calls=%async_computation.1 | async-start | bytes 5767168 | tf_op jit(solution)/shard_map/all_to_all | solution.py:125
  88.9 1.1 reduce-window.14
  90.1 0.2 slice_reduce_fusion.1
  90.5 3.0 scatter_custom_fusion.2
  93.5 0.4 select_reduce_fusion
  94.0 0.9 cosine_convert_fusion.1
  94.9 10.1 %cosine_convert_fusion = bf16[512,10,128]{2,0,1:T(8,128)(2,1)} fusion(f32[128]{0:T(128)S(1)} %copy-done.17, f32[128]{0:T(128)S(1)} %copy-done.18, f32[512,10]{0,1:T(8,128)S(1)} %subtract_convert_fusion), kind=kLoop, calls=%fused_computation.20 | loop fusion | flops 1966080 | bytes 1332224 | tf_op jit(solution)/shard_map/convert_element_type | solution.py:170
  105.0 15.5 %all-to-all-done.1 = bf16[8,1408,128]{2,1,0:T(8,128)(2,1)} async-done(((bf16[8,1408,128]{2,1,0:T(8,128)(2,1)}), bf16[8,1408,128]{2,1,0:T(8,128)(2,1)}, u32[]{:S(2)}, u32[]{:S(2)}) %all-to-all-start.1) | async-done | bytes 2883616 | tf_op jit(solution)/shard_map/all_to_all | solution.py:125
  120.5 6.9 %all-to-all-start.3 = ((s32[8,1,128]{2,1,0:T(1,128)}), s32[8,1,128]{2,1,0:T(1,128)S(1)}, u32[]{:S(2)}, u32[]{:S(2)}) async-start(s32[8,1,128]{2,1,0:T(1,128)} %bitcast.18), calls=%async_computation.3 | async-start | bytes 8192 | tf_op jit(solution)/shard_map/all_to_all | solution.py:115
  127.4 13.4 %gather_fusion.1 = bf16[5632,128]{1,0:T(8,128)(2,1)} fusion(bf16[11264,128]{1,0:T(8,128)(2,1)} %bitcast.15, s32[6144]{0:T(1024)S(1)} %pad_clamp_fusion), kind=kCustom, calls=%fused_computation.1 | custom fusion | bytes 2906112 | tf_op jit(solution)/shard_map/gather | solution.py:126
  140.7 3.7 %reshape.238 = bf16[512,11,128]{2,1,0:T(8,128)(2,1)} reshape(bf16[5632,128]{1,0:T(8,128)(2,1)} %gather_fusion.1) | data formatting | bytes 2883584 | tf_op jit(solution)/shard_map/reshape | solution.py:126
  144.4 1.4 slice.78
  145.9 3.2 scatter_custom_fusion.1
  149.0 4.2 %all-to-all-start.2 = ((bf16[8,128,256]{2,1,0:T(8,128)(2,1)}), bf16[8,128,256]{2,1,0:T(8,128)(2,1)S(1)}, u32[]{:S(2)}, u32[]{:S(2)}) async-start(bf16[8,128,256]{2,1,0:T(8,128)(2,1)} %bitcast.16), calls=%async_computation.2 | async-start | bytes 1048576 | tf_op jit(solution)/shard_map/all_to_all | solution.py:137
  153.3 3.2 gather_fusion.2
  156.5 1.5 fusion.65
  158.0 2.6 slice.85
  160.6 1.4 copy.95
  162.0 0.4 convolution_add_fusion
  162.4 1.0 copy-done.4
  163.4 1.1 fusion.21
  164.4 4.4 %all-to-all-start.4 = ((bf16[8,128,128]{2,1,0:T(8,128)(2,1)}), bf16[8,128,128]{2,1,0:T(8,128)(2,1)S(1)}, u32[]{:S(2)}, u32[]{:S(2)}) async-start(bf16[8,128,128]{2,1,0:T(8,128)(2,1)} %bitcast.21), calls=%async_computation.4 | async-start | bytes 524288 | tf_op jit(solution)/shard_map/all_to_all | solution.py:145
  168.8 2.6 fusion.4
  171.4 2.3 copy-done.2
  173.7 0.7 all-to-all-done.4
  174.5 1.3 gather_fusion.3
  175.8 1.3 gather_fusion.4
  177.2 0.2 fusion.66
  177.4 4.0 %multiply_reduce_fusion.3 = (f32[512,2,10]{0,1,2:T(2,128)S(1)}, f32[512,10,128]{0,2,1:T(8,128)}) fusion(f32[512,2,64]{0,2,1:T(8,128)S(1)} %bitcast.119, f32[512,10,256]{0,2,1:T(8,128)} %copy-done.2), kind=kLoop, calls=%fused_computation.19 | loop fusion | flops 1300480 | bytes 5545984 | tf_op jit(solution)/shard_map/jvp(ehd,enhd->ehn)/dot_general | solution.py:51
  181.6 0.3 multiply_reduce_fusion.2
  182.1 0.2 copy-done.10
  182.3 0.1 copy-done.21
  182.4 1.0 fusion.62
  183.4 0.9 fusion.14
  184.3 0.2 fusion.67
  184.6 2.6 broadcast_multiply_fusion.1
  187.4 0.4 broadcast_multiply_fusion
  187.9 0.9 fusion.15
  188.8 0.4 copy-done.6
  189.2 1.6 fusion.11
  190.8 0.7 all-gather.2.cloned.1.call-update
  191.6 10.6 %all_gather.6 = s32[4096]{0:T(1024)S(1)} all-gather(s32[1024]{0:T(1024)S(1)} %get-tuple-element.27), channel_id=1, replica_groups=mesh['node'=8,'batch'=4] {'batch'}, dimensions={0}, use_global_device_ids=true | all-gather | bytes 20480 | tf_op jit(solution)/shard_map/all_gather | solution.py:159
  202.1 26.3 %all-reduce.9.cloned.1.call-done = (f32[128,128]{1,0:T(8,128)}, f32[256,256]{1,0:T(8,128)}, f32[256,128]{1,0:T(8,128)}) async-done(((f32[128,128]{1,0:T(8,128)}, f32[256,256]{1,0:T(8,128)}, f32[256,128]{1,0:T(8,128)}), (f32[128,128]{1,0:T(8,128)}, f32[256,256]{1,0:T(8,128)}, f32[256,128]{1,0:T(8,128)})) %all-reduce.9.cloned.1.call-update) | async-done | bytes 458768 | tf_op jit(solution)/shard_map/psum | solution.py:184
  228.5 24.3 %scatter_custom_fusion.3 = s32[8193]{0:T(1024)S(1)} fusion(s32[4096]{0:T(1024)S(1)} %get-tuple-element.26, s32[4096]{0:T(1024)S(1)} %all_gather.6, s32[]{:T(128)} %constant.30.clone.1), kind=kCustom, calls=%fused_computation.96 | custom fusion | flops 4096 | bytes 32776 | tf_op jit(solution)/shard_map/scatter-max | solution.py:163
  252.8 23.0 %gather_fusion.5 = s32[4096]{0:T(1024)S(1)} fusion(s32[8193]{0:T(1024)S(1)} %scatter_custom_fusion.3, s32[4096]{0:T(1024)S(1)} %get-tuple-element.25), kind=kCustom, calls=%fused_computation.5 | custom fusion | bytes 49152 | tf_op jit(solution)/shard_map/gather | solution.py:164
  275.9 8.2 %psum.62 = f32[128]{0:T(128)S(1)} all-reduce(f32[128]{0:T(128)S(1)} %get-tuple-element.14), channel_id=1, replica_groups=mesh['node'=8,'batch'=4] {'batch'}, use_global_device_ids=true, to_apply=%region_24.25 | all-reduce | flops 128 | bytes 1024 | tf_op jit(solution)/shard_map/psum | solution.py:184
  284.0 17.4 %psum.63 = f32[128]{0:T(128)} all-reduce(f32[128]{0:T(128)S(1)} %psum.62), channel_id=1, replica_groups=mesh['node'=8,'batch'=4] {'node'}, use_global_device_ids=true, to_apply=%region_25.26 | all-reduce | flops 128 | bytes 1024 | tf_op jit(solution)/shard_map/psum | solution.py:184
  301.5 12.5 %scatter_fusion = bf16[8192,128]{1,0:T(8,128)(2,1)S(1)} fusion(bf16[8192,128]{1,0:T(8,128)(2,1)S(1)} %copy.112, s32[4096]{0:T(1024)S(1)} %compare_select_fusion.2, bf16[4096,128]{1,0:T(8,128)(2,1)} %all-gather.2.cloned.1.call-done), kind=kCustom, calls=%fused_computation.10 | custom fusion | bytes 3162112 | tf_op jit(solution)/shard_map/scatter | solution.py:166
  314.0 2.8 all-reduce.7.cloned.1.call-done
  316.8 1.5 copy.113
  318.2 1.7 copy.114
  319.9 1.6 copy.115
  (88 shorter events, 1.6 us)
Async XLA Ops:
  7.2 154.8 %copy-start = (bf16[256,384]{1,0:T(8,128)(2,1)S(1)}, bf16[256,384]{1,0:T(8,128)(2,1)}, u32[]{:S(2)}) copy-start(bf16[256,384]{1,0:T(8,128)(2,1)} %param.28) | copy-start | bytes 589828
  7.2 1.7 copy-start.9
  7.2 5.7 %copy-start.12 = (s32[512,11]{0,1:T(8,128)S(1)}, s32[512,11]{0,1:T(8,128)}, u32[]{:S(2)}) copy-start(s32[512,11]{0,1:T(8,128)} %param.22) | copy-start | bytes 67588
  83.6 5.3 %copy-start.11 = (s32[512,1]{0,1:T(1,128)S(1)}, s32[512,1]{0,1:T(1,128)}, u32[]{:S(2)}) copy-start(s32[512,1]{0,1:T(1,128)} %param.19) | copy-start | bytes 6148
  83.6 6.8 %copy-start.15 = (s32[512]{0:T(512)S(1)}, s32[512]{0:T(512)}, u32[]{:S(2)}) copy-start(s32[512]{0:T(512)} %param.20) | copy-start | bytes 6148
  83.6 10.3 %copy-start.16 = (s32[512]{0:T(512)S(1)}, s32[512]{0:T(512)}, u32[]{:S(2)}) copy-start(s32[512]{0:T(512)} %param.23) | copy-start | bytes 6148
  83.6 10.3 %copy-start.19 = (s32[512]{0:T(512)S(1)}, s32[512]{0:T(512)}, u32[]{:S(2)}) copy-start(s32[512]{0:T(512)} %param.24) | copy-start | bytes 6148
  83.6 10.3 %copy-start.13 = (s32[512,10]{0,1:T(8,128)S(1)}, s32[512,10]{0,1:T(8,128)}, u32[]{:S(2)}) copy-start(s32[512,10]{0,1:T(8,128)} %param.25) | copy-start | bytes 61444
  83.6 10.3 %copy-start.17 = (f32[128]{0:T(128)S(1)}, f32[128]{0:T(128)}, u32[]{:S(2)}) copy-start(f32[128]{0:T(128)} %param.27) | copy-start | bytes 1540
  83.6 10.3 %copy-start.18 = (f32[128]{0:T(128)S(1)}, f32[128]{0:T(128)}, u32[]{:S(2)}) copy-start(f32[128]{0:T(128)} %param.26) | copy-start | bytes 1540
  83.6 43.7 %copy-start.20 = (f32[512]{0:T(512)S(1)}, f32[512]{0:T(512)}, u32[]{:S(2)}) copy-start(f32[512]{0:T(512)} %param.30) | copy-start | bytes 6148
  83.7 36.8 %all-to-all-start.1 = ((bf16[8,1408,128]{2,1,0:T(8,128)(2,1)}), bf16[8,1408,128]{2,1,0:T(8,128)(2,1)}, u32[]{:S(2)}, u32[]{:S(2)}) async-start(bf16[8,1408,128]{2,1,0:T(8,128)(2,1)} %bitcast.114), calls=%async_computation.1 | async-start | bytes 5767168 | tf_op jit(solution)/shard_map/all_to_all | solution.py:125
  120.5 28.5 %all-to-all-start.3 = ((s32[8,1,128]{2,1,0:T(1,128)}), s32[8,1,128]{2,1,0:T(1,128)S(1)}, u32[]{:S(2)}, u32[]{:S(2)}) async-start(s32[8,1,128]{2,1,0:T(1,128)} %bitcast.18), calls=%async_computation.3 | async-start | bytes 8192 | tf_op jit(solution)/shard_map/all_to_all | solution.py:115
  144.4 12.0 %copy-start.8 = (bf16[128,384]{1,0:T(8,128)(2,1)S(1)}, bf16[128,384]{1,0:T(8,128)(2,1)}, u32[]{:S(2)}) copy-start(bf16[128,384]{1,0:T(8,128)(2,1)} %param.29) | copy-start | bytes 294916
  149.0 12.9 %all-to-all-start.2 = ((bf16[8,128,256]{2,1,0:T(8,128)(2,1)}), bf16[8,128,256]{2,1,0:T(8,128)(2,1)S(1)}, u32[]{:S(2)}, u32[]{:S(2)}) async-start(bf16[8,128,256]{2,1,0:T(8,128)(2,1)} %bitcast.16), calls=%async_computation.2 | async-start | bytes 1048576 | tf_op jit(solution)/shard_map/all_to_all | solution.py:137
  162.0 1.4 copy-start.4
  163.4 5.5 %copy-start.7 = (bf16[256,256]{1,0:T(8,128)(2,1)S(1)}, bf16[256,256]{1,0:T(8,128)(2,1)}, u32[]{:S(2)}) copy-start(bf16[256,256]{1,0:T(8,128)(2,1)} %param.32) | copy-start | bytes 393220
  164.4 10.0 %all-to-all-start.4 = ((bf16[8,128,128]{2,1,0:T(8,128)(2,1)}), bf16[8,128,128]{2,1,0:T(8,128)(2,1)S(1)}, u32[]{:S(2)}, u32[]{:S(2)}) async-start(bf16[8,128,128]{2,1,0:T(8,128)(2,1)} %bitcast.21), calls=%async_computation.4 | async-start | bytes 524288 | tf_op jit(solution)/shard_map/all_to_all | solution.py:145
  168.8 59.7 %all-reduce.9.cloned.1.call-start = ((), (), s32[]{:S(2)}) async-start(), calls=%async_computation.7 | async-start | bytes 917504 | tf_op jit(solution)/shard_map/psum | solution.py:184
  171.4 2.3 copy-start.2
  173.7 3.4 %copy-start.14 = (bf16[128,128]{1,0:T(8,128)(2,1)S(1)}, bf16[128,128]{1,0:T(8,128)(2,1)}, u32[]{:S(2)}) copy-start(bf16[128,128]{1,0:T(8,128)(2,1)} %param.31) | copy-start | bytes 98308
  177.4 4.2 %slice-start = ((f32[512,10,256]{0,2,1:T(8,128)}), f32[512,10,128]{0,2,1:T(8,128)S(1)}, s32[]{:S(2)}) async-start(f32[512,10,256]{0,2,1:T(8,128)} %copy-done.2), calls=%async_computation.8 | async-start | bytes 5242880 | tf_op jit(solution)/shard_map/jvp()/slice | solution.py:50
  181.4 0.8 copy-start.10
  181.4 1.0 copy-start.21
  181.4 1.0 copy-start.22
  184.6 2.8 copy-start.3
  187.4 1.3 copy-start.5
  187.4 1.7 copy-start.6
  190.8 110.7 %all-gather.2.cloned.1.call-start = ((), (), s32[]{:S(2)}) async-start(), calls=%async_computation.5 | async-start | bytes 1310720 | tf_op jit(solution)/shard_map/all_gather | solution.py:158
  191.5 125.2 %all-reduce.7.cloned.1.call-start = ((), (), s32[]{:S(2)}) async-start(), calls=%async_computation.6 | async-start | bytes 917504 | tf_op jit(solution)/shard_map/psum | solution.py:184
  313.9 7.5 %copy-start.1 = (bf16[8192,128]{1,0:T(8,128)(2,1)}, bf16[8192,128]{1,0:T(8,128)(2,1)S(1)}, u32[]{:S(2)}) copy-start(bf16[8192,128]{1,0:T(8,128)(2,1)S(1)} %scatter_fusion) | copy-start | bytes 6291460
Sparse Core Ops, SparseCore 0:
  190.9 37.5 all-reduce.8
  230.7 28.5 all-gather.1
  263.0 53.6 all-reduce.6
